TPU v7x, 256 devices: a whole 4x4x8 slice. The times are simulated.
256 devices in a mesh: section: 2 (over z_lo), dp: 128 (over x, y, z_hi, core).
Axes of the slice: x: 4, y: 4, z: 8 (z_hi: 4, z_lo: 2; z = z_hi * 2 + z_lo), core: 2. Of those that a mesh axis runs over, the one named last changes fastest.
Arguments:
- tokens: bfloat16 [98304, 832], P('dp'), may hold values from -6 to 6
- out_grad: bfloat16 [98304, 832], P('dp'), may hold values from -0.059814453 to 0.059814453
- boundary: int32 [1], replicated, may hold values from 0 to 11
- up_old: float32 [12, 2, 832, 2048], P('section', None, None, 'dp'), may hold values from -0.21875 to 0.21875
- down_old: float32 [12, 2, 2048, 832], P('section', None, 'dp'), may hold values from -0.09375 to 0.09375
- up_mom: float32 [12, 2, 832, 2048], P('section', None, None, 'dp'), may hold values from -2 to 2
- up_var: float32 [12, 2, 832, 2048], P('section', None, None, 'dp'), may hold values from 0.01 to 1
- down_mom: float32 [12, 2, 2048, 832], P('section', None, 'dp'), may hold values from -2 to 2
- down_var: float32 [12, 2, 2048, 832], P('section', None, 'dp'), may hold values from 0.01 to 1
Outputs:
- mixed: bfloat16 [98304, 832], P('dp')
- up_new: float32 [2, 832, 2048], P('section', None, 'dp')
- up_mom_new: float32 [2, 832, 2048], P('section', None, 'dp')
- up_var_new: float32 [2, 832, 2048], P('section', None, 'dp')
- down_new: float32 [2, 2048, 832], P('section', 'dp')
- down_mom_new: float32 [2, 2048, 832], P('section', 'dp')
- down_var_new: float32 [2, 2048, 832], P('section', 'dp')
All inputs are finite; a program needn't handle non-finite values.
Results may differ from a plain program's by a relative error of at most 0.00115.
The roundings to bfloat16 on the way count: a program that leaves them out, or rounds other values in their place, can miss the bound.
Values may be sent and summed in bfloat16 or wider, within the bound.
A program may use at most 128 MiB of HBM per device.

v0:
```python
import math

import jax
import jax.numpy as jnp
from jax import lax
from jax.sharding import PartitionSpec as P

root_half = 1.0 / math.sqrt(2.0)
root_circle = 1.0 / math.sqrt(2.0 * math.pi)
first_fix = 1.0 - 0.9**10
second_fix = 1.0 - 0.999**10


def from_root(value, axis, source):
    kept = jnp.where(lax.axis_index(axis) == source, value, 0).astype(value.dtype)
    return lax.psum(kept, axis)


def gelu_value(value):
    return 0.5 * value * (1.0 + lax.erf(value * root_half))


def gelu_slope(value):
    return (
        0.5 * (1.0 + lax.erf(value * root_half))
        + value * jnp.exp(-0.5 * value * value) * root_circle
    )


def layer_norm(tokens):
    wide = tokens.astype(jnp.float32)
    center = wide - jnp.mean(wide, axis=1, keepdims=True)
    spread = jnp.mean(center * center, axis=1, keepdims=True)
    return (center * lax.rsqrt(spread + 1e-06)).astype(jnp.bfloat16)


def adam_update(weight, moment, second, grad):
    moment_new = 0.9 * moment + 0.1 * grad
    second_new = 0.999 * second + 0.001 * grad * grad
    stride = moment_new / first_fix / (jnp.sqrt(second_new / second_fix) + 1e-08)
    return (weight - 0.001 * stride, moment_new, second_new)


def local(tokens, out_grad, boundary, up_old, down_old, up_mom, up_var, down_mom, down_var):
    active = boundary[0]
    layer_count = up_old.shape[0]
    owner = active // layer_count
    local_slot = active % layer_count
    own_half = lax.axis_index("section")
    bundle = (up_old, up_mom, up_var, down_old, down_mom, down_var)
    picked = tuple(
        (lax.dynamic_index_in_dim(item, local_slot, 0, keepdims=False) for item in bundle)
    )
    moved = jax.tree.map(lambda part: from_root(part, "section", owner), picked)
    fresh = tuple((lax.dynamic_slice_in_dim(item, own_half, 1, 0) for item in moved))
    up_w, up_m, up_v, down_w, down_m, down_v = fresh
    normed = layer_norm(tokens)
    up_piece = up_w[0].astype(jnp.bfloat16)
    down_piece = down_w[0].astype(jnp.bfloat16)
    pre = jnp.dot(
        normed,
        lax.all_gather(up_piece, "dp", axis=1, tiled=True),
        preferred_element_type=jnp.float32,
    )
    act = gelu_value(pre).astype(jnp.bfloat16)
    columns = act
    partial_sum = jnp.dot(
        columns,
        lax.all_gather(down_piece, "dp", axis=0, tiled=True),
        preferred_element_type=jnp.float32,
    )
    back = lax.dot_general(
        out_grad,
        lax.all_gather(down_piece, "dp", axis=0, tiled=True),
        (((1,), (1,)), ((), ())),
        preferred_element_type=jnp.float32,
    )
    branch = lax.psum(partial_sum, "section")
    mixed = (tokens.astype(jnp.float32) + branch).astype(jnp.bfloat16)
    slope = (back * gelu_slope(pre)).astype(jnp.bfloat16)
    columns = act
    grad_down = lax.psum_scatter(
        lax.dot_general(
            columns, out_grad, (((0,), (0,)), ((), ())), preferred_element_type=jnp.float32
        ),
        "dp",
        scatter_dimension=0,
        tiled=True,
    )
    columns = slope
    grad_up_rows = lax.psum_scatter(
        lax.dot_general(
            columns, normed, (((0,), (0,)), ((), ())), preferred_element_type=jnp.float32
        ),
        "dp",
        scatter_dimension=0,
        tiled=True,
    )
    grad_up = jnp.transpose(grad_up_rows)[None]
    up_new, up_mom_new, up_var_new = adam_update(up_w, up_m, up_v, grad_up)
    down_new, down_mom_new, down_var_new = adam_update(down_w, down_m, down_v, grad_down[None])
    return (mixed, up_new, up_mom_new, up_var_new, down_new, down_mom_new, down_var_new)


def solution(mesh):
    in_specs = (
        P("dp", None),
        P("dp", None),
        P(),
        P("section", None, None, "dp"),
        P("section", None, "dp", None),
        P("section", None, None, "dp"),
        P("section", None, None, "dp"),
        P("section", None, "dp", None),
        P("section", None, "dp", None),
    )
    out_specs = (
        P("dp", None),
        P("section", None, "dp"),
        P("section", None, "dp"),
        P("section", None, "dp"),
        P("section", "dp", None),
        P("section", "dp", None),
        P("section", "dp", None),
    )
    return jax.shard_map(local, mesh=mesh, in_specs=in_specs, out_specs=out_specs, check_vma=False)
```

profile of v0, /device:TPU:1, one launch (start us, length us, event | category | flops | bytes accessed | tf_op | source)
XLA Modules:
  0.0 1731.5 jit_solution(7783419146104466301)
XLA Ops:
  7.2 0.0 copy-start
  7.2 0.0 copy-start.1
  7.2 0.0 all-reduce.7.cloned.1.call-start
  8.1 1.6 select_bitcast_fusion.4
  9.6 1.6 select_bitcast_fusion.5
  11.2 0.0 all-reduce.7.cloned.1.call-update
  11.2 0.0 all-gather.5.cloned.1.call-start
  11.3 37.6 %all-reduce.7.cloned.1.call-done = (f32[2,832,16]{1,2,0:T(8,128)}, f32[2,16,832]{2,1,0:T(8,128)}) async-done(((f32[2,832,16]{1,2,0:T(8,128)}, f32[2,16,832]{2,1,0:T(8,128)}), (f32[2,832,16]{1,2,0:T(8,128)}, f32[2,16,832]{2,1,0:T(8,128)})) %all-reduce.7.cloned.1.call-update) | async-done | bytes 213008 | tf_op jit(solution)/shard_map/psum | solution.py:16
  48.9 1.4 dynamic-slice_convert_fusion.1
  50.3 0.0 all-gather.5.cloned.1.call-update
  50.4 0.0 all-gather.7.cloned.1.call-start
  50.4 1.4 dynamic-slice_convert_fusion
  51.8 0.0 all-gather.7.cloned.1.call-update
  51.9 0.0 all-reduce.5.cloned.1.call-start
  51.9 1.7 select_bitcast_fusion
  53.6 1.7 select_bitcast_fusion.2
  55.2 1.5 convert_reduce_fusion
  56.8 0.0 copy-done.1
  56.8 0.4 fusion.13
  57.2 75.5 %all-gather.5.cloned.1.call-done = bf16[1,832,2048]{1,2,0:T(8,128)(2,1)} async-done(((bf16[1,832,16]{1,2,0:T(8,128)(2,1)}), bf16[1,832,2048]{1,2,0:T(8,128)(2,1)}) %all-gather.5.cloned.1.call-update) | async-done | bytes 3407888 | tf_op jit(solution)/shard_map/all_gather | solution.py:62
  132.7 8.0 multiply_convert_fusion
  140.7 72.7 %all-gather.7.cloned.1.call-done = bf16[1,2048,832]{2,1,0:T(8,128)(2,1)} async-done(((bf16[1,16,832]{2,1,0:T(8,128)(2,1)}), bf16[1,2048,832]{2,1,0:T(8,128)(2,1)}) %all-gather.7.cloned.1.call-update) | async-done | bytes 3407888 | tf_op jit(solution)/shard_map/all_gather | solution.py:69
  213.4 7.4 fusion.7
  220.8 0.0 all-reduce.5.cloned.1.call-update
  220.8 0.0 reduce-scatter.5.cloned.1.call-start
  220.8 0.0 copy-done
  220.8 7.4 fusion.30
  228.3 0.0 reduce-scatter.5.cloned.1.call-update
  228.3 0.2 reduce-scatter.3.cloned.1.call-start
  228.5 13.5 fusion.17
  242.0 0.0 reduce-scatter.3.cloned.1.call-update
  242.1 0.0 copy-start.3
  242.1 0.0 copy-start.2
  242.1 71.5 %all-reduce.5.cloned.1.call-done = (f32[768,832]{0,1:T(8,128)}, f32[2,832,16]{1,2,0:T(8,128)}, f32[2,832,16]{1,2,0:T(8,128)}, f32[2,16,832]{2,1,0:T(8,128)}, f32[2,16,832]{2,1,0:T(8,128)}) async-done(((f32[768,832]{0,1:T(8,128)}, f32[2,832,16]{1,2,0:T(8,128)}, f32[2,832,16]{1,2,0:T(8,128)}, f32[2,16,832]{2,1,0:T(8,128)}, f32[2,16,832]{2,1,0:T(8,128)}), (f32[768,832]{0,1:T(8,128)}, f32[2,832,16]{1,2,0:T(8,128)}, ...) | async-done | bytes 2981904 | tf_op jit(solution)/shard_map/psum | solution.py:78
  313.6 0.0 copy-start.6
  313.6 0.0 copy-start.7
  313.6 0.0 copy-start.4
  313.6 3.1 fusion.15
  316.7 702.6 %reduce-scatter.5.cloned.1.call-done = f32[16,832]{1,0:T(8,128)} async-done(((f32[2048,832]{1,0:T(8,128)}), f32[16,832]{1,0:T(8,128)}) %reduce-scatter.5.cloned.1.call-update) | async-done | bytes 53264 | tf_op jit(solution)/shard_map/reduce_scatter | solution.py:82
  1019.3 0.0 copy-done.3
  1019.3 0.0 copy-done.6
  1019.3 0.0 copy-done.7
  1019.3 1.5 multiply_subtract_fusion
  1020.8 702.3 %reduce-scatter.3.cloned.1.call-done = f32[16,832]{1,0:T(8,128)} async-done(((f32[2048,832]{1,0:T(8,128)}), f32[16,832]{1,0:T(8,128)}) %reduce-scatter.3.cloned.1.call-update) | async-done | bytes 53264 | tf_op jit(solution)/shard_map/reduce_scatter | solution.py:91
  1723.2 0.0 copy-done.2
  1723.2 0.0 copy-done.4
  1723.2 0.0 copy-done.5
  1723.2 1.5 multiply_subtract_fusion.1
  (3 shorter events, 0.0 us)
Async XLA Ops:
  7.2 213.7 %copy-start = (bf16[768,832]{0,1:T(8,128)(2,1)S(1)}, bf16[768,832]{0,1:T(8,128)(2,1)}, u32[]{:S(2)}) copy-start(bf16[768,832]{0,1:T(8,128)(2,1)} %param.10) | copy-start | bytes 3833860
  7.2 49.6 %copy-start.1 = (bf16[768,832]{0,1:T(8,128)(2,1)S(1)}, bf16[768,832]{0,1:T(8,128)(2,1)}, u32[]{:S(2)}) copy-start(bf16[768,832]{0,1:T(8,128)(2,1)} %param.9) | copy-start | bytes 3833860
  7.2 41.7 %all-reduce.7.cloned.1.call-start = ((), (), s32[]{:S(2)}) async-start(), calls=%async_computation.7 | async-start | bytes 458752 | tf_op jit(solution)/shard_map/psum | solution.py:16
  11.2 121.5 %all-gather.5.cloned.1.call-start = ((), (), s32[]{:S(2)}) async-start(), calls=%async_computation.4 | async-start | bytes 3698688 | tf_op jit(solution)/shard_map/all_gather | solution.py:62
  50.4 163.0 %all-gather.7.cloned.1.call-start = ((), (), s32[]{:S(2)}) async-start(), calls=%async_computation.5 | async-start | bytes 3698688 | tf_op jit(solution)/shard_map/all_gather | solution.py:69
  51.9 261.7 %all-reduce.5.cloned.1.call-start = ((), (), s32[]{:S(2)}) async-start(), calls=%async_computation.6 | async-start | bytes 6029312 | tf_op jit(solution)/shard_map/psum | solution.py:78
  220.8 798.5 %reduce-scatter.5.cloned.1.call-start = ((), (), s32[]{:S(2)}) async-start(), calls=%async_computation.3 | async-start | bytes 7397376 | tf_op jit(solution)/shard_map/reduce_scatter | solution.py:82
  228.3 1494.8 %reduce-scatter.3.cloned.1.call-start = ((), (), s32[]{:S(2)}) async-start(), calls=%async_computation.2 | async-start | bytes 7397376 | tf_op jit(solution)/shard_map/reduce_scatter | solution.py:91
  242.1 777.3 %copy-start.3 = (f32[2,16,832]{2,1,0:T(8,128)S(1)}, f32[2,16,832]{2,1,0:T(8,128)}, u32[]{:S(2)}) copy-start(f32[2,16,832]{2,1,0:T(8,128)} %get-tuple-element.13) | copy-start | bytes 319492
  242.1 1481.1 %copy-start.2 = (f32[2,832,16]{1,2,0:T(8,128)S(1)}, f32[2,832,16]{1,2,0:T(8,128)}, u32[]{:S(2)}) copy-start(f32[2,832,16]{1,2,0:T(8,128)} %get-tuple-element.12) | copy-start | bytes 319492
  313.6 705.7 %copy-start.6 = (f32[2,16,832]{2,1,0:T(8,128)S(1)}, f32[2,16,832]{2,1,0:T(8,128)}, u32[]{:S(2)}) copy-start(f32[2,16,832]{2,1,0:T(8,128)} %get-tuple-element.10) | copy-start | bytes 319492
  313.6 705.7 %copy-start.7 = (f32[2,16,832]{2,1,0:T(8,128)S(1)}, f32[2,16,832]{2,1,0:T(8,128)}, u32[]{:S(2)}) copy-start(f32[2,16,832]{2,1,0:T(8,128)} %get-tuple-element.11) | copy-start | bytes 319492
  313.6 1409.5 %copy-start.4 = (f32[2,832,16]{1,2,0:T(8,128)S(1)}, f32[2,832,16]{1,2,0:T(8,128)}, u32[]{:S(2)}) copy-start(f32[2,832,16]{1,2,0:T(8,128)} %get-tuple-element.8) | copy-start | bytes 319492
  313.6 1409.5 %copy-start.5 = (f32[2,832,16]{1,2,0:T(8,128)S(1)}, f32[2,832,16]{1,2,0:T(8,128)}, u32[]{:S(2)}) copy-start(f32[2,832,16]{1,2,0:T(8,128)} %get-tuple-element.9) | copy-start | bytes 319492
Sparse Core Ops, SparseCore 0:
  11.3 37.5 all-reduce.6
  52.9 79.7 all-gather.4
  136.7 76.6 all-gather.6
  220.9 92.6 all-reduce.4
  316.1 703.1 reduce-scatter.4
  1021.7 701.4 reduce-scatter.2
where the time goes:
time: 1740 us; the launch traced here: 1730 us
  waiting for transfers between devices  1660 us (95%)
  matrix products  36.4 us (2%)
    reduce_scatter x1, waiting for transfers between devices, local(): lax.psum_scatter(lax.dot_general(columns, out_grad, (((0,), (0,)), ((), (...  703 us
    reduce_scatter x1, waiting for transfers between devices, local(): lax.psum_scatter(lax.dot_general(columns, normed, (((0,), (0,)), ((), ())...  702 us
    all_gather x1, waiting for transfers between devices, local(): lax.all_gather(up_piece, 'dp', axis=1, tiled=True)  75.5 us
    all_gather x1, waiting for transfers between devices, local(): lax.all_gather(down_piece, 'dp', axis=0, tiled=True)  72.7 us
    psum x1, waiting for transfers between devices, local(): branch = lax.psum(partial_sum, 'section')  71.5 us
    psum x1, waiting for transfers between devices, from_root(): return lax.psum(kept, axis)  37.6 us
  transfers between devices with their start and end apart: 6, of which 6 were waited for; matrix products, arithmetic and copies ran while one was open for 2% of the time, Pallas kernels for 0%

commit v1 on v0

v1 whole, which is shorter than its diff:
```python
import functools
import math

import jax
import jax.numpy as jnp
from jax import lax
from jax.experimental import pallas as pl
from jax.experimental.pallas import tpu as pltpu
from jax.sharding import PartitionSpec as P

root_half = 1.0 / math.sqrt(2.0)
root_circle = 1.0 / math.sqrt(2.0 * math.pi)
first_fix = 1.0 - 0.9**10
second_fix = 1.0 - 0.999**10

D = 832
ROWS = 16
TOK = 768
HALF_TOK = TOK // 2
UNITS = 64 * ROWS
CLASS = 16 * ROWS
F32 = jnp.float32
BF16 = jnp.bfloat16


def dot(a, b, ca, cb):
    return lax.dot_general(a, b, (((ca,), (cb,)), ((), ())), preferred_element_type=F32)


def gelu_both(value):
    both = 1.0 + lax.erf(value * root_half)
    return 0.5 * value * both, 0.5 * both + value * jnp.exp(-0.5 * value * value) * root_circle


def layer_norm(tokens):
    wide = tokens.astype(F32)
    center = wide - jnp.mean(wide, axis=0, keepdims=True)
    spread = jnp.mean(center * center, axis=0, keepdims=True)
    return (center * lax.rsqrt(spread + 1e-06)).astype(BF16)


def adam_update(weight, moment, second, grad):
    moment_new = 0.9 * moment + 0.1 * grad
    second_new = 0.999 * second + 0.001 * grad * grad
    stride = moment_new / first_fix / (jnp.sqrt(second_new / second_fix) + 1e-08)
    return (weight - 0.001 * stride, moment_new, second_new)


def flip1(v):
    return v + 1 - 2 * lax.rem(v, 2)


def flip2(v):
    return lax.rem(v + 2, 4)


def flip3(v):
    return 3 - v


def kernel(
    boundary,
    tok_in,
    og_in,
    up_w_in,
    down_w_in,
    up_m_in,
    up_v_in,
    down_m_in,
    down_v_in,
    mixed_out,
    up_w_out,
    up_m_out,
    up_v_out,
    down_w_out,
    down_m_out,
    down_v_out,
    up_w,
    down_w,
    up_m,
    down_m,
    up_v,
    down_v,
    pick_send,
    pick_recv,
    picked,
    tok,
    nrm,
    og,
    w1,
    w2,
    act,
    gate,
    slope,
    psend,
    pown,
    precv,
    zrecv,
    mix,
    gd,
    gu,
    rd,
    ru,
    zd,
    zu,
    local_sem,
    send_sem,
    recv_sem,
):
    s = lax.axis_index("section")
    d = lax.axis_index("dp")
    x, y, z, c = lax.div(d, 32), lax.rem(lax.div(d, 8), 4), lax.rem(lax.div(d, 2), 4), lax.rem(d, 2)
    core = {"dp": d + 1 - 2 * c}
    pair = {"section": 1 - s}
    xy = (
        {"dp": d + (flip1(x) - x) * 32},
        {"dp": d + (flip3(x) - x) * 32},
        {"dp": d + (flip1(y) - y) * 8},
        {"dp": d + (flip3(y) - y) * 8},
    )
    zs = (
        {"dp": d + (flip1(z) - z) * 2},
        {"dp": d + (flip3(z) - z) * 2},
        {"dp": d + (flip2(z) - z) * 2},
    )
    state = (up_w, down_w, up_m, down_m, up_v, down_v)
    active = boundary[0]
    slot = lax.rem(active, 6)
    owner = lax.div(active, 6)

    count = [0]
    started = []

    def send(src, dst, dev):
        i = count[0]
        count[0] += 1
        copy = pltpu.make_async_remote_copy(
            src_ref=src,
            dst_ref=dst,
            send_sem=send_sem.at[i],
            recv_sem=recv_sem.at[i],
            device_id=dev,
            device_id_type=pl.DeviceIdType.MESH,
        )
        copy.start()
        started.append(copy)
        return copy

    mine = pl.ds(pl.multiple_of(s * HALF_TOK, 128), HALF_TOK)
    other = pl.ds(pl.multiple_of((1 - s) * HALF_TOK, 128), HALF_TOK)
    first, second = pl.ds(0, HALF_TOK), pl.ds(HALF_TOK, HALF_TOK)

    def fetch(i, src, dst):
        copy = pltpu.make_async_copy(src, dst, local_sem.at[i])
        copy.start()
        return copy

    get_w = [fetch(0, up_w_in, up_w), fetch(1, down_w_in, down_w)]
    get_tok = [
        fetch(2, tok_in.at[:, mine], tok.at[:, first]),
        fetch(3, tok_in.at[:, other], tok.at[:, second]),
    ]
    get_og = [
        fetch(4, og_in.at[:, mine], og.at[:, pl.ds(0, HALF_TOK)]),
        fetch(5, og_in.at[:, other], og.at[:, pl.ds(HALF_TOK, HALF_TOK)]),
    ]
    get_mv = [
        fetch(6, up_m_in, up_m),
        fetch(7, down_m_in, down_m),
        fetch(8, up_v_in, up_v),
        fetch(9, down_v_in, down_v),
    ]

    barrier = pltpu.get_barrier_semaphore()
    peers = (core, pair) + xy + zs
    for peer in peers:
        pl.semaphore_signal(barrier, inc=1, device_id=peer, device_id_type=pl.DeviceIdType.MESH)
    pl.semaphore_wait(barrier, len(peers))

    def swap(i):
        pick_send[i] = state[i][slot, 1 - s]
        return send(pick_send.at[i], pick_recv.at[i], pair)

    def settle(i, copy):
        copy.wait_recv()
        picked[i] = jnp.where(owner == s, state[i][slot, s], pick_recv[i])

    for copy in get_w:
        copy.wait()
    moved = [swap(0), swap(1)]
    for copy in get_og:
        copy.wait()
    og_swap = send(og.at[:, pl.ds(0, TOK)], og.at[:, pl.ds(TOK, TOK)], core)
    for copy in get_tok:
        copy.wait()

    def norm_half(h):
        @pl.loop(0, HALF_TOK // 128)
        def _(i):
            at = pl.ds(pl.multiple_of(h * HALF_TOK + i * 128, 128), 128)
            nrm[:, at] = layer_norm(tok[:, at])

    norm_half(0)
    weights = (w1, w2)
    gathered = {}
    for m in (0, 1):
        settle(m, moved[m])
        weights[m][pl.ds(0, ROWS), :] = picked[m].astype(BF16)
        for q in (1, 2, 3):
            gathered[m, q, -1] = send(
                weights[m].at[pl.ds(0, ROWS), :], weights[m].at[pl.ds(q * CLASS, ROWS), :], zs[q - 1]
            )
    norm_half(1)
    nrm_swap = send(nrm.at[:, pl.ds(0, TOK)], nrm.at[:, pl.ds(TOK, TOK)], core)

    for j in range(4):
        n = ROWS << j
        for m in (0, 1):
            for q in range(4):
                if j > 0 or q > 0:
                    gathered[m, q, j - 1].wait_recv()
                gathered[m, q, j] = send(
                    weights[m].at[pl.ds(q * CLASS, n), :],
                    weights[m].at[pl.ds(q * CLASS + n, n), :],
                    xy[(q + j) % 4],
                )
        if j == 0:
            for copy in get_mv:
                copy.wait()
            moved += [swap(i) for i in (2, 3, 4, 5)]

    og_swap.wait_recv()
    nrm_swap.wait_recv()
    for q in range(4):
        gathered[0, q, 3].wait_recv()

    def forward(t):
        cols = pl.ds(t * TOK, TOK)

        @pl.loop(0, 2)
        def _(i):
            rows = pl.ds(pl.multiple_of(i * 512, 512), 512)
            value, rate = gelu_both(dot(w1[rows, :], nrm[:, cols], 1, 0))
            act[rows, cols] = value.astype(BF16)
            gate[rows, cols] = rate

    forward(1)
    for q in range(4):
        gathered[1, q, 3].wait_recv()

    def branch(block):
        return dot(w2[...], act[:, pl.ds(block * HALF_TOK, HALF_TOK)], 0, 0)

    psend[1] = branch(3)
    core_swap1 = send(psend.at[1], precv.at[1], core)
    psend[0] = branch(2)
    core_swap0 = send(psend.at[0], precv.at[0], core)
    forward(0)
    pown[1] = branch(1)
    core_swap1.wait_recv()
    pown[1] += precv[1]
    pair_swap = send(pown.at[1], zrecv, pair)

    sums = {}

    def begin(name, grad, recv, q):
        top = CLASS // 2
        sums[name, q, 3] = send(
            grad.at[pl.ds(q * CLASS + top, top), :], recv.at[pl.ds(q * 240, top), :], xy[(q + 3) % 4]
        )

    def advance(name, grad, recv, zrecv_, j):
        n = ROWS << j
        at = (16 - (2 << j)) * ROWS
        for q in range(4):
            base, low = q * CLASS, q * 240 + at
            sums[name, q, j].wait_recv()
            if j > 0:
                h = n // 2
                grad[pl.ds(base + h, h), :] += recv[pl.ds(low + h, h), :]
                sums[name, q, j - 1] = send(
                    grad.at[pl.ds(base + h, h), :],
                    recv.at[pl.ds(low + n, h), :],
                    xy[(q + j - 1) % 4],
                )
                grad[pl.ds(base, h), :] += recv[pl.ds(low, h), :]
            else:
                grad[pl.ds(base, n), :] += recv[pl.ds(low, n), :]
                if q > 0:
                    sums[name, q, -1] = send(grad.at[pl.ds(base, n), :], zrecv_.at[q - 1], zs[q - 1])

    def finish(name, grad, zrecv_):
        total = grad[pl.ds(0, ROWS), :]
        for q in (1, 2, 3):
            sums[name, q, -1].wait_recv()
            total = total + zrecv_[q - 1]
        return total

    for q in range(4):
        rows = pl.ds(q * CLASS, CLASS)
        gd[rows, :] = dot(act[rows, :], og[...], 1, 1)
        begin("d", gd, rd, q)

    @pl.loop(0, 4)
    def _(i):
        rows = pl.ds(pl.multiple_of(lax.div(i, 2) * 512, 512), 512)
        cols = pl.ds(pl.multiple_of(lax.rem(i, 2) * TOK, 128), TOK)
        back = dot(w2[rows, :], og[:, cols], 1, 0)
        slope[rows, cols] = (back * gate[rows, cols]).astype(BF16)

    for q in range(4):
        rows = pl.ds(q * CLASS, CLASS)
        gu[rows, :] = dot(slope[rows, :], nrm[...], 1, 1)
        begin("u", gu, ru, q)

    pown[0] = branch(0)
    core_swap0.wait_recv()
    pown[0] += precv[0]

    advance("d", gd, rd, zd, 3)
    advance("d", gd, rd, zd, 2)
    for i in (2, 3, 4, 5):
        settle(i, moved[i])
    advance("u", gu, ru, zu, 3)
    advance("d", gd, rd, zd, 1)
    advance("u", gu, ru, zu, 2)
    advance("d", gd, rd, zd, 0)

    pair_swap.wait_recv()
    mix[0] = (tok[:, first].astype(F32) + (pown[0] + zrecv[...])).astype(BF16)
    mix_swap = send(mix.at[0], mix.at[1], pair)
    put0 = pltpu.make_async_copy(mix.at[0], mixed_out.at[:, mine], local_sem.at[10])
    put0.start()

    advance("u", gu, ru, zu, 1)
    advance("u", gu, ru, zu, 0)
    down_w_out[...], down_m_out[...], down_v_out[...] = adam_update(
        picked[1], picked[3], picked[5], finish("d", gd, zd)
    )
    up_w_out[...], up_m_out[...], up_v_out[...] = adam_update(
        picked[0], picked[2], picked[4], finish("u", gu, zu)
    )
    mix_swap.wait_recv()
    put1 = pltpu.make_async_copy(mix.at[1], mixed_out.at[:, other], local_sem.at[11])
    put1.start()
    put0.wait()
    put1.wait()
    for copy in started:
        copy.wait_send()


COPIES = 6 + 2 + 6 + 32 + 4 + 38


def local(tokens, out_grad, boundary, up_old, down_old, up_mom, up_var, down_mom, down_var):
    layers = up_old.shape[0]
    hbm = pl.BlockSpec(memory_space=pl.ANY)
    vmem = pl.BlockSpec(memory_space=pltpu.VMEM)
    piece = jax.ShapeDtypeStruct((ROWS, D), F32)
    swap = lambda a: jnp.swapaxes(a, -1, -2)
    V = pltpu.VMEM
    results = pl.pallas_call(
        kernel,
        out_shape=[jax.ShapeDtypeStruct((D, TOK), BF16)] + [piece] * 6,
        in_specs=[pl.BlockSpec(memory_space=pltpu.SMEM)] + [hbm] * 8,
        out_specs=[hbm] + [vmem] * 6,
        scratch_shapes=[
            *[V((layers, 2, ROWS, D), F32)] * 6,
            V((6, ROWS, D), F32),
            V((6, ROWS, D), F32),
            V((6, ROWS, D), F32),
            V((D, TOK), BF16),
            V((D, 2 * TOK), BF16),
            V((D, 2 * TOK), BF16),
            V((UNITS, D), BF16),
            V((UNITS, D), BF16),
            V((UNITS, 2 * TOK), BF16),
            V((UNITS, 2 * TOK), F32),
            V((UNITS, 2 * TOK), BF16),
            V((2, D, HALF_TOK), F32),
            V((2, D, HALF_TOK), F32),
            V((2, D, HALF_TOK), F32),
            V((D, HALF_TOK), F32),
            V((2, D, HALF_TOK), BF16),
            V((UNITS, D), F32),
            V((UNITS, D), F32),
            V((4 * 240, D), F32),
            V((4 * 240, D), F32),
            V((3, ROWS, D), F32),
            V((3, ROWS, D), F32),
            pltpu.SemaphoreType.DMA((12,)),
            pltpu.SemaphoreType.DMA((COPIES,)),
            pltpu.SemaphoreType.DMA((COPIES,)),
        ],
        compiler_params=pltpu.CompilerParams(
            collective_id=0, has_side_effects=True, vmem_limit_bytes=60 * 2**20
        ),
        name="block_step",
    )(
        boundary,
        swap(tokens),
        swap(out_grad),
        swap(up_old),
        down_old,
        swap(up_mom),
        swap(up_var),
        down_mom,
        down_var,
    )
    mixed, up_w, up_m, up_v, down_w, down_m, down_v = results
    return (
        swap(mixed),
        swap(up_w)[None],
        swap(up_m)[None],
        swap(up_v)[None],
        down_w[None],
        down_m[None],
        down_v[None],
    )


def solution(mesh):
    in_specs = (
        P("dp", None),
        P("dp", None),
        P(),
        P("section", None, None, "dp"),
        P("section", None, "dp", None),
        P("section", None, None, "dp"),
        P("section", None, None, "dp"),
        P("section", None, "dp", None),
        P("section", None, "dp", None),
    )
    out_specs = (
        P("dp", None),
        P("section", None, "dp"),
        P("section", None, "dp"),
        P("section", None, "dp"),
        P("section", "dp", None),
        P("section", "dp", None),
        P("section", "dp", None),
    )
    return jax.shard_map(local, mesh=mesh, in_specs=in_specs, out_specs=out_specs, check_vma=False)
```

time: 1740 us -> 120 us (0.07)
  the two profiles are of different devices: /device:TPU:1 before, /device:TPU:8 now
where the time goes in v1:
time: 120 us
  Pallas kernels  112 us (93%)
  local copies, waits for them, and re-layouts  6.28 us (5%)
  between operations  1.34 us (1%)
    pallas_call x1, Pallas kernels, local(): pl.pallas_call(kernel, out_shape=[jax.ShapeDtypeStruct((D, TOK), BF16)] +...  112 us
    unnamed x19, local copies, waits for them, and re-layouts  6.28 us

profile of v1, /device:TPU:8, one launch (start us, length us, event | category | flops | bytes accessed | tf_op | source)
XLA Modules:
  0.0 119.9 jit_solution(11656265053477726791)
XLA Ops:
  1.3 112.3 %block_step.1 = (bf16[832,768]{1,0:T(8,128)(2,1)}, f32[16,832]{1,0:T(8,128)}, f32[16,832]{1,0:T(8,128)}, f32[16,832]{1,0:T(8,128)}, f32[16,832]{1,0:T(8,128)}, /*index=5*/f32[16,832]{1,0:T(8,128)}, f32[16,832]{1,0:T(8,128)}) custom-call(s32[1]{0:T(128)S(6)} %copy.23.boundary, bf16[832,768]{1,0:T(8,128)(2,1)} %bitcast.19, bf16[832,768]{1,0:T(8,128)(2,1)} %bitcast.20, ...), custom_call_target="tpu_custom_call" | custom-call | tf_op jit(solution)/shard_map/block_step/pallas_call | solution.py:362
  113.6 0.0 copy-start.5
  113.6 0.0 copy-start.4
  113.6 0.0 copy-start.3
  113.6 0.0 copy-start.2
  113.6 0.0 copy-start.1
  113.6 0.0 copy-start
  113.7 2.5 %copy.24 = bf16[768,832]{0,1:T(8,128)(2,1)} copy(bf16[768,832]{0,1:T(8,128)(2,1)} %bitcast.18) | data formatting | bytes 2555904
  116.2 0.0 copy-done.5
  116.2 0.6 copy.25
  116.8 0.0 copy-done.4
  116.8 0.6 copy.26
  117.4 0.0 copy-done.3
  117.4 0.6 copy.27
  118.1 0.0 copy-done.2
  118.1 0.6 copy.28
  118.7 0.0 copy-done.1
  118.7 0.6 copy.29
  119.3 0.0 copy-done
  119.3 0.6 copy.30
Async XLA Ops:
  113.6 2.6 %copy-start.5 = (f32[16,832]{1,0:T(8,128)S(1)}, f32[16,832]{1,0:T(8,128)}, u32[]{:S(2)}) copy-start(f32[16,832]{1,0:T(8,128)} %get-tuple-element.15) | copy-start | bytes 159748
  113.6 3.2 %copy-start.4 = (f32[16,832]{1,0:T(8,128)S(1)}, f32[16,832]{1,0:T(8,128)}, u32[]{:S(2)}) copy-start(f32[16,832]{1,0:T(8,128)} %get-tuple-element.16) | copy-start | bytes 159748
  113.6 3.8 %copy-start.3 = (f32[16,832]{1,0:T(8,128)S(1)}, f32[16,832]{1,0:T(8,128)}, u32[]{:S(2)}) copy-start(f32[16,832]{1,0:T(8,128)} %get-tuple-element.17) | copy-start | bytes 159748
  113.6 4.4 %copy-start.2 = (f32[16,832]{1,0:T(8,128)S(1)}, f32[16,832]{1,0:T(8,128)}, u32[]{:S(2)}) copy-start(f32[16,832]{1,0:T(8,128)} %get-tuple-element.18) | copy-start | bytes 159748
  113.6 5.0 %copy-start.1 = (f32[16,832]{1,0:T(8,128)S(1)}, f32[16,832]{1,0:T(8,128)}, u32[]{:S(2)}) copy-start(f32[16,832]{1,0:T(8,128)} %get-tuple-element.19) | copy-start | bytes 159748
  113.6 5.7 %copy-start = (f32[16,832]{1,0:T(8,128)S(1)}, f32[16,832]{1,0:T(8,128)}, u32[]{:S(2)}) copy-start(f32[16,832]{1,0:T(8,128)} %get-tuple-element.20) | copy-start | bytes 159748

commit v2 on v1

--- a/solution.py
+++ b/solution.py
@@ -18,7 +18,8 @@
 TOK = 768
 HALF_TOK = TOK // 2
 UNITS = 64 * ROWS
-CLASS = 16 * ROWS
+CLASS = 8 * ROWS
+LATE = UNITS // 2
 F32 = jnp.float32
 BF16 = jnp.bfloat16
 
@@ -69,21 +70,19 @@
     down_m_in,
     down_v_in,
     mixed_out,
-    up_w_out,
-    up_m_out,
-    up_v_out,
-    down_w_out,
-    down_m_out,
-    down_v_out,
+    state_out,
     up_w,
     down_w,
     up_m,
     down_m,
     up_v,
     down_v,
+    bpiece,
+    brecv,
     pick_send,
     pick_recv,
     picked,
+    fresh,
     tok,
     nrm,
     og,
@@ -123,6 +122,7 @@
         {"dp": d + (flip3(z) - z) * 2},
         {"dp": d + (flip2(z) - z) * 2},
     )
+    pair_zs = tuple({"section": 1 - s, "dp": peer["dp"]} for peer in zs)
     state = (up_w, down_w, up_m, down_m, up_v, down_v)
     active = boundary[0]
     slot = lax.rem(active, 6)
@@ -156,13 +156,17 @@
         return copy
 
     get_w = [fetch(0, up_w_in, up_w), fetch(1, down_w_in, down_w)]
+    barrier = pltpu.get_barrier_semaphore()
+    peers = (core, pair) + xy + zs + pair_zs
+    for peer in peers:
+        pl.semaphore_signal(barrier, inc=1, device_id=peer, device_id_type=pl.DeviceIdType.MESH)
     get_tok = [
         fetch(2, tok_in.at[:, mine], tok.at[:, first]),
         fetch(3, tok_in.at[:, other], tok.at[:, second]),
     ]
     get_og = [
-        fetch(4, og_in.at[:, mine], og.at[:, pl.ds(0, HALF_TOK)]),
-        fetch(5, og_in.at[:, other], og.at[:, pl.ds(HALF_TOK, HALF_TOK)]),
+        fetch(4, og_in.at[:, mine], og.at[:, first]),
+        fetch(5, og_in.at[:, other], og.at[:, second]),
     ]
     get_mv = [
         fetch(6, up_m_in, up_m),
@@ -171,103 +175,107 @@
         fetch(9, down_v_in, down_v),
     ]
 
-    barrier = pltpu.get_barrier_semaphore()
-    peers = (core, pair) + xy + zs
-    for peer in peers:
-        pl.semaphore_signal(barrier, inc=1, device_id=peer, device_id_type=pl.DeviceIdType.MESH)
+    def norm(i):
+        at = pl.ds(i * 128, 128)
+        nrm[:, at] = layer_norm(tok[:, at])
+
+    for copy in get_w:
+        copy.wait()
+    for m in (0, 1):
+        bpiece[0, m] = state[m][slot, s].astype(BF16)
+        bpiece[1, m] = state[m][slot, 1 - s].astype(BF16)
     pl.semaphore_wait(barrier, len(peers))
-
-    def swap(i):
-        pick_send[i] = state[i][slot, 1 - s]
-        return send(pick_send.at[i], pick_recv.at[i], pair)
-
-    def settle(i, copy):
-        copy.wait_recv()
-        picked[i] = jnp.where(owner == s, state[i][slot, s], pick_recv[i])
-
-    for copy in get_w:
-        copy.wait()
-    moved = [swap(0), swap(1)]
+    offers = [send(bpiece.at[1], brecv.at[0], pair)]
+    offers += [send(bpiece.at[0], brecv.at[q], zs[q - 1]) for q in (1, 2, 3)]
+    offers += [send(bpiece.at[1], brecv.at[q + 3], pair_zs[q - 1]) for q in (1, 2, 3)]
     for copy in get_og:
         copy.wait()
     og_swap = send(og.at[:, pl.ds(0, TOK)], og.at[:, pl.ds(TOK, TOK)], core)
     for copy in get_tok:
         copy.wait()
-
-    def norm_half(h):
-        @pl.loop(0, HALF_TOK // 128)
-        def _(i):
-            at = pl.ds(pl.multiple_of(h * HALF_TOK + i * 128, 128), 128)
-            nrm[:, at] = layer_norm(tok[:, at])
-
-    norm_half(0)
+    norm(0)
     weights = (w1, w2)
     gathered = {}
+
+    def spread(m, q, j):
+        n, at = ROWS << j, q * CLASS
+        if j > 0:
+            gathered[m, q, j - 1].wait_recv()
+        gathered[m, q, j] = send(
+            weights[m].at[pl.ds(at, n), :],
+            weights[m].at[pl.ds(at + n if j < 3 else LATE + at, n), :],
+            xy[(q + j) % 4],
+        )
+
+    for q in range(4):
+        if q > 0:
+            offers[q].wait_recv()
+            offers[q + 3].wait_recv()
+        else:
+            offers[0].wait_recv()
+        for m in (0, 1):
+            near = bpiece[0, m] if q == 0 else brecv[q, m]
+            far = brecv[0, m] if q == 0 else brecv[q + 3, m]
+            weights[m][pl.ds(q * CLASS, ROWS), :] = jnp.where(owner == s, near, far)
+            spread(m, q, 0)
+    norm(1)
+    norm(2)
+    nrm_swaps = [send(nrm.at[:, first], nrm.at[:, pl.ds(TOK, HALF_TOK)], core)]
     for m in (0, 1):
-        settle(m, moved[m])
-        weights[m][pl.ds(0, ROWS), :] = picked[m].astype(BF16)
-        for q in (1, 2, 3):
-            gathered[m, q, -1] = send(
-                weights[m].at[pl.ds(0, ROWS), :], weights[m].at[pl.ds(q * CLASS, ROWS), :], zs[q - 1]
-            )
-    norm_half(1)
-    nrm_swap = send(nrm.at[:, pl.ds(0, TOK)], nrm.at[:, pl.ds(TOK, TOK)], core)
-
-    for j in range(4):
-        n = ROWS << j
-        for m in (0, 1):
-            for q in range(4):
-                if j > 0 or q > 0:
-                    gathered[m, q, j - 1].wait_recv()
-                gathered[m, q, j] = send(
-                    weights[m].at[pl.ds(q * CLASS, n), :],
-                    weights[m].at[pl.ds(q * CLASS + n, n), :],
-                    xy[(q + j) % 4],
-                )
-        if j == 0:
-            for copy in get_mv:
-                copy.wait()
-            moved += [swap(i) for i in (2, 3, 4, 5)]
-
-    og_swap.wait_recv()
-    nrm_swap.wait_recv()
+        for q in range(4):
+            spread(m, q, 1)
+    norm(3)
+    for copy in get_mv:
+        copy.wait()
+    for i in range(6):
+        pick_send[i] = state[i][slot, 1 - s]
+    moved = send(pick_send, pick_recv, pair)
+    norm(4)
+    for m in (0, 1):
+        for q in range(4):
+            spread(m, q, 2)
+    norm(5)
+    nrm_swaps.append(send(nrm.at[:, second], nrm.at[:, pl.ds(TOK + HALF_TOK, HALF_TOK)], core))
+    for q in range(4):
+        spread(0, q, 3)
+
+    def forward(part, t):
+        rows, cols = pl.ds(part * LATE, LATE), pl.ds(t * TOK, TOK)
+        value, rate = gelu_both(dot(w1[rows, :], nrm[:, cols], 1, 0))
+        act[rows, cols] = value.astype(BF16)
+        gate[rows, cols] = rate
+
+    def backward(part):
+        @pl.loop(0, 2)
+        def _(t):
+            rows, cols = pl.ds(part * LATE, LATE), pl.ds(pl.multiple_of(t * TOK, 128), TOK)
+            back = dot(w2[rows, :], og[:, cols], 1, 0)
+            slope[rows, cols] = (back * gate[rows, cols]).astype(BF16)
+
+    def branch(block):
+        return dot(w2[...], act[:, pl.ds(block * HALF_TOK, HALF_TOK)], 0, 0)
+
+    forward(0, 0)
+    for copy in nrm_swaps:
+        copy.wait_recv()
+    forward(0, 1)
     for q in range(4):
         gathered[0, q, 3].wait_recv()
-
-    def forward(t):
-        cols = pl.ds(t * TOK, TOK)
-
-        @pl.loop(0, 2)
-        def _(i):
-            rows = pl.ds(pl.multiple_of(i * 512, 512), 512)
-            value, rate = gelu_both(dot(w1[rows, :], nrm[:, cols], 1, 0))
-            act[rows, cols] = value.astype(BF16)
-            gate[rows, cols] = rate
-
-    forward(1)
     for q in range(4):
-        gathered[1, q, 3].wait_recv()
-
-    def branch(block):
-        return dot(w2[...], act[:, pl.ds(block * HALF_TOK, HALF_TOK)], 0, 0)
-
-    psend[1] = branch(3)
-    core_swap1 = send(psend.at[1], precv.at[1], core)
-    psend[0] = branch(2)
-    core_swap0 = send(psend.at[0], precv.at[0], core)
-    forward(0)
-    pown[1] = branch(1)
-    core_swap1.wait_recv()
-    pown[1] += precv[1]
-    pair_swap = send(pown.at[1], zrecv, pair)
+        spread(1, q, 3)
+    forward(1, 0)
+    forward(1, 1)
 
     sums = {}
-
-    def begin(name, grad, recv, q):
-        top = CLASS // 2
-        sums[name, q, 3] = send(
-            grad.at[pl.ds(q * CLASS + top, top), :], recv.at[pl.ds(q * 240, top), :], xy[(q + 3) % 4]
-        )
+    early, late = pl.ds(0, LATE), pl.ds(LATE, LATE)
+
+    def begin(name, grad, recv):
+        for q in range(4):
+            sums[name, q, 3] = send(
+                grad.at[pl.ds(LATE + q * CLASS, CLASS), :],
+                recv.at[pl.ds(q * 240, CLASS), :],
+                xy[(q + 3) % 4],
+            )
 
     def advance(name, grad, recv, zrecv_, j):
         n = ROWS << j
@@ -296,76 +304,88 @@
             total = total + zrecv_[q - 1]
         return total
 
+    og_swap.wait_recv()
+    gd[late, :] = dot(act[late, :], og[...], 1, 1)
+    begin("d", gd, rd)
     for q in range(4):
-        rows = pl.ds(q * CLASS, CLASS)
-        gd[rows, :] = dot(act[rows, :], og[...], 1, 1)
-        begin("d", gd, rd, q)
-
-    @pl.loop(0, 4)
-    def _(i):
-        rows = pl.ds(pl.multiple_of(lax.div(i, 2) * 512, 512), 512)
-        cols = pl.ds(pl.multiple_of(lax.rem(i, 2) * TOK, 128), TOK)
-        back = dot(w2[rows, :], og[:, cols], 1, 0)
-        slope[rows, cols] = (back * gate[rows, cols]).astype(BF16)
-
-    for q in range(4):
-        rows = pl.ds(q * CLASS, CLASS)
-        gu[rows, :] = dot(slope[rows, :], nrm[...], 1, 1)
-        begin("u", gu, ru, q)
-
+        gathered[1, q, 3].wait_recv()
+
+    psend[1] = branch(3)
+    core_swap1 = send(psend.at[1], precv.at[1], core)
+    pown[1] = branch(1)
+    gd[early, :] = dot(act[early, :], og[...], 1, 1)
+    core_swap1.wait_recv()
+    pown[1] += precv[1]
+    pair_swap = send(pown.at[1], zrecv, pair)
+    backward(1)
+    gu[late, :] = dot(slope[late, :], nrm[...], 1, 1)
+    begin("u", gu, ru)
+    psend[0] = branch(2)
+    core_swap0 = send(psend.at[0], precv.at[0], core)
     pown[0] = branch(0)
+    advance("d", gd, rd, zd, 3)
+    backward(0)
+    gu[early, :] = dot(slope[early, :], nrm[...], 1, 1)
     core_swap0.wait_recv()
     pown[0] += precv[0]
-
-    advance("d", gd, rd, zd, 3)
     advance("d", gd, rd, zd, 2)
-    for i in (2, 3, 4, 5):
-        settle(i, moved[i])
     advance("u", gu, ru, zu, 3)
     advance("d", gd, rd, zd, 1)
     advance("u", gu, ru, zu, 2)
+    moved.wait_recv()
+    for i in range(6):
+        picked[i] = jnp.where(owner == s, state[i][slot, s], pick_recv[i])
     advance("d", gd, rd, zd, 0)
+    advance("u", gu, ru, zu, 1)
 
     pair_swap.wait_recv()
     mix[0] = (tok[:, first].astype(F32) + (pown[0] + zrecv[...])).astype(BF16)
     mix_swap = send(mix.at[0], mix.at[1], pair)
-    put0 = pltpu.make_async_copy(mix.at[0], mixed_out.at[:, mine], local_sem.at[10])
-    put0.start()
-
-    advance("u", gu, ru, zu, 1)
+    puts = [pltpu.make_async_copy(mix.at[0], mixed_out.at[:, mine], local_sem.at[10])]
+    puts[0].start()
     advance("u", gu, ru, zu, 0)
-    down_w_out[...], down_m_out[...], down_v_out[...] = adam_update(
-        picked[1], picked[3], picked[5], finish("d", gd, zd)
-    )
-    up_w_out[...], up_m_out[...], up_v_out[...] = adam_update(
-        picked[0], picked[2], picked[4], finish("u", gu, zu)
-    )
+    fresh[3], fresh[4], fresh[5] = adam_update(picked[1], picked[3], picked[5], finish("d", gd, zd))
+    fresh[0], fresh[1], fresh[2] = adam_update(picked[0], picked[2], picked[4], finish("u", gu, zu))
+    puts.append(pltpu.make_async_copy(fresh, state_out, local_sem.at[12]))
+    puts[1].start()
     mix_swap.wait_recv()
-    put1 = pltpu.make_async_copy(mix.at[1], mixed_out.at[:, other], local_sem.at[11])
-    put1.start()
-    put0.wait()
-    put1.wait()
+    puts.append(pltpu.make_async_copy(mix.at[1], mixed_out.at[:, other], local_sem.at[11]))
+    puts[2].start()
+    for copy in puts:
+        copy.wait()
     for copy in started:
         copy.wait_send()
 
 
-COPIES = 6 + 2 + 6 + 32 + 4 + 38
+COPIES = 7 + 1 + 2 + 1 + 32 + 4 + 38
+
+
+def hand_out(mixed_in, state_in, mixed_out, *rest):
+    outs, sem = rest[:6], rest[6]
+    copies = [pltpu.make_async_copy(mixed_in, mixed_out, sem.at[6])]
+    copies += [pltpu.make_async_copy(state_in.at[i], outs[i], sem.at[i]) for i in range(6)]
+    for copy in copies:
+        copy.start()
+    for copy in copies:
+        copy.wait()
 
 
 def local(tokens, out_grad, boundary, up_old, down_old, up_mom, up_var, down_mom, down_var):
     layers = up_old.shape[0]
     hbm = pl.BlockSpec(memory_space=pl.ANY)
-    vmem = pl.BlockSpec(memory_space=pltpu.VMEM)
-    piece = jax.ShapeDtypeStruct((ROWS, D), F32)
     swap = lambda a: jnp.swapaxes(a, -1, -2)
     V = pltpu.VMEM
+    mixed_type = jax.ShapeDtypeStruct((D, TOK), BF16)
     results = pl.pallas_call(
         kernel,
-        out_shape=[jax.ShapeDtypeStruct((D, TOK), BF16)] + [piece] * 6,
+        out_shape=[mixed_type, jax.ShapeDtypeStruct((6, ROWS, D), F32)],
         in_specs=[pl.BlockSpec(memory_space=pltpu.SMEM)] + [hbm] * 8,
-        out_specs=[hbm] + [vmem] * 6,
+        out_specs=[hbm] * 2,
         scratch_shapes=[
             *[V((layers, 2, ROWS, D), F32)] * 6,
+            V((2, 2, ROWS, D), BF16),
+            V((7, 2, ROWS, D), BF16),
+            V((6, ROWS, D), F32),
             V((6, ROWS, D), F32),
             V((6, ROWS, D), F32),
             V((6, ROWS, D), F32),
@@ -388,7 +408,7 @@
             V((4 * 240, D), F32),
             V((3, ROWS, D), F32),
             V((3, ROWS, D), F32),
-            pltpu.SemaphoreType.DMA((12,)),
+            pltpu.SemaphoreType.DMA((13,)),
             pltpu.SemaphoreType.DMA((COPIES,)),
             pltpu.SemaphoreType.DMA((COPIES,)),
         ],
@@ -407,7 +427,15 @@
         down_mom,
         down_var,
     )
-    mixed, up_w, up_m, up_v, down_w, down_m, down_v = results
+    mixed, up_w, up_m, up_v, down_w, down_m, down_v = pl.pallas_call(
+        hand_out,
+        out_shape=[mixed_type] + [jax.ShapeDtypeStruct((ROWS, D), F32)] * 6,
+        in_specs=[hbm] * 2,
+        out_specs=[hbm] * 7,
+        scratch_shapes=[pltpu.SemaphoreType.DMA((7,))],
+        compiler_params=pltpu.CompilerParams(vmem_limit_bytes=60 * 2**20),
+        name="hand_out",
+    )(*results)
     return (
         swap(mixed),
         swap(up_w)[None],

time: 120 us -> 165 us (1.38)
  the two profiles are of different devices: /device:TPU:8 before, /device:TPU:1 now
where the time goes in v2:
time: 165 us; the launch traced here: 163 us
  Pallas kernels  162 us (98%)
    pallas_call x1, Pallas kernels, local(): pl.pallas_call(kernel, out_shape=[mixed_type, jax.ShapeDtypeStruct((6, RO...  112 us
    pallas_call x1, Pallas kernels, local(): pl.pallas_call(hand_out, out_shape=[mixed_type] + [jax.ShapeDtypeStruct((...  50.3 us

profile of v2, /device:TPU:1, one launch (start us, length us, event | category | flops | bytes accessed | tf_op | source)
XLA Modules:
  0.0 163.4 jit_solution(10220280008956962723)
XLA Ops:
  1.3 111.6 %block_step.1 = (bf16[832,768]{1,0:T(8,128)(2,1)}, f32[6,16,832]{2,1,0:T(8,128)}) custom-call(s32[1]{0:T(128)S(6)} %copy.16.boundary, bf16[832,768]{1,0:T(8,128)(2,1)} %bitcast.18, bf16[832,768]{1,0:T(8,128)(2,1)} %bitcast.19, f32[6,2,16,832]{3,2,1,0:T(8,128)} %bitcast.20, f32[6,2,16,832]{3,2,1,0:T(8,128)} %down_w_in.1, f32[6,2,16,832]{3,2,1,0:T(8,128)} %bitcast.21, ...), custom_call_target="tpu_custom_call" | custom-call | tf_op jit(solution)/shard_map/block_step/pallas_call | solution.py:379
  112.9 50.3 %hand_out.1 = (bf16[832,768]{1,0:T(8,128)(2,1)}, f32[16,832]{1,0:T(8,128)}, f32[16,832]{1,0:T(8,128)}, f32[16,832]{1,0:T(8,128)}, f32[16,832]{1,0:T(8,128)}, /*index=5*/f32[16,832]{1,0:T(8,128)}, f32[16,832]{1,0:T(8,128)}) custom-call(bf16[832,768]{1,0:T(8,128)(2,1)} %get-tuple-element.16.mixed_in, f32[6,16,832]{2,1,0:T(8,128)} %get-tuple-element.17.state_in), custom_call_target="tpu_custom_call" | custom-call | tf_op jit(solution)/shard_map/hand_out/pallas_call | solution.py:430

commit v3 on v2

--- a/solution.py
+++ b/solution.py
@@ -45,6 +45,38 @@
     second_new = 0.999 * second + 0.001 * grad * grad
     stride = moment_new / first_fix / (jnp.sqrt(second_new / second_fix) + 1e-08)
     return (weight - 0.001 * stride, moment_new, second_new)
+
+
+def tiles(width):
+    return [pl.ds(at, min(128, width - at)) for at in range(0, width, 128)]
+
+
+def encode(x, code, scale):
+    n, w = x.shape
+    top = jnp.max(jnp.abs(x).reshape(n // 8, 8, w), axis=0)
+    best = top[:, :128]
+    for at in range(128, w - 127, 128):
+        best = jnp.maximum(best, top[:, at : at + 128])
+    rest = w % 128
+    if rest:
+        best = jnp.concatenate([jnp.maximum(best[:, :rest], top[:, w - rest :]), best[:, rest:]], axis=1)
+    unit = jnp.maximum(best, 1e-30) * (1.0 / 32760.0)
+    scale[...] = unit
+    per = 1.0 / unit
+    for cols in tiles(w):
+        part = x[:, cols.start : cols.start + cols.size].reshape(n // 8, 8, cols.size)
+        part = jnp.round(part * per[None, :, : cols.size])
+        code[:, cols] = part.astype(jnp.int32).astype(jnp.int16).reshape(n, cols.size)
+
+
+def decode(code, scale, cols):
+    part = code[:, cols].astype(jnp.int32).astype(F32)
+    n, w = part.shape
+    return (part.reshape(n // 8, 8, w) * scale[:, pl.ds(0, w)][None]).reshape(n, w)
+
+
+def decode_wide(code, scale):
+    return jnp.concatenate([decode(code, scale, cols) for cols in tiles(code.shape[1])], axis=1)
 
 
 def flip1(v):
@@ -94,14 +126,17 @@
     psend,
     pown,
     precv,
-    zrecv,
+    pair_code,
+    pair_scale,
+    pair_code_in,
+    pair_scale_in,
     mix,
     gd,
     gu,
-    rd,
-    ru,
-    zd,
-    zu,
+    sum_code,
+    sum_scale,
+    sum_code_in,
+    sum_scale_in,
     local_sem,
     send_sem,
     recv_sem,
@@ -122,7 +157,6 @@
         {"dp": d + (flip3(z) - z) * 2},
         {"dp": d + (flip2(z) - z) * 2},
     )
-    pair_zs = tuple({"section": 1 - s, "dp": peer["dp"]} for peer in zs)
     state = (up_w, down_w, up_m, down_m, up_v, down_v)
     active = boundary[0]
     slot = lax.rem(active, 6)
@@ -157,7 +191,7 @@
 
     get_w = [fetch(0, up_w_in, up_w), fetch(1, down_w_in, down_w)]
     barrier = pltpu.get_barrier_semaphore()
-    peers = (core, pair) + xy + zs + pair_zs
+    peers = (core, pair) + xy + zs
     for peer in peers:
         pl.semaphore_signal(barrier, inc=1, device_id=peer, device_id_type=pl.DeviceIdType.MESH)
     get_tok = [
@@ -185,21 +219,15 @@
         bpiece[0, m] = state[m][slot, s].astype(BF16)
         bpiece[1, m] = state[m][slot, 1 - s].astype(BF16)
     pl.semaphore_wait(barrier, len(peers))
-    offers = [send(bpiece.at[1], brecv.at[0], pair)]
-    offers += [send(bpiece.at[0], brecv.at[q], zs[q - 1]) for q in (1, 2, 3)]
-    offers += [send(bpiece.at[1], brecv.at[q + 3], pair_zs[q - 1]) for q in (1, 2, 3)]
-    for copy in get_og:
-        copy.wait()
-    og_swap = send(og.at[:, pl.ds(0, TOK)], og.at[:, pl.ds(TOK, TOK)], core)
+    offers = [send(bpiece.at[1, m], brecv.at[m], pair) for m in (0, 1)]
     for copy in get_tok:
         copy.wait()
-    norm(0)
     weights = (w1, w2)
     gathered = {}
 
     def spread(m, q, j):
         n, at = ROWS << j, q * CLASS
-        if j > 0:
+        if j > 0 or q > 0:
             gathered[m, q, j - 1].wait_recv()
         gathered[m, q, j] = send(
             weights[m].at[pl.ds(at, n), :],
@@ -207,16 +235,20 @@
             xy[(q + j) % 4],
         )
 
-    for q in range(4):
-        if q > 0:
-            offers[q].wait_recv()
-            offers[q + 3].wait_recv()
-        else:
-            offers[0].wait_recv()
-        for m in (0, 1):
-            near = bpiece[0, m] if q == 0 else brecv[q, m]
-            far = brecv[0, m] if q == 0 else brecv[q + 3, m]
-            weights[m][pl.ds(q * CLASS, ROWS), :] = jnp.where(owner == s, near, far)
+    for m in (0, 1):
+        offers[m].wait_recv()
+        weights[m][pl.ds(0, ROWS), :] = jnp.where(owner == s, bpiece[0, m], brecv[m])
+        for q in (1, 2, 3):
+            gathered[m, q, -1] = send(
+                weights[m].at[pl.ds(0, ROWS), :], weights[m].at[pl.ds(q * CLASS, ROWS), :], zs[q - 1]
+            )
+        spread(m, 0, 0)
+    for copy in get_og:
+        copy.wait()
+    og_swap = send(og.at[:, pl.ds(0, TOK)], og.at[:, pl.ds(TOK, TOK)], core)
+    norm(0)
+    for m in (0, 1):
+        for q in (1, 2, 3):
             spread(m, q, 0)
     norm(1)
     norm(2)
@@ -267,107 +299,136 @@
     forward(1, 1)
 
     sums = {}
+    grads = (gd, gu)
     early, late = pl.ds(0, LATE), pl.ds(LATE, LATE)
 
-    def begin(name, grad, recv):
+    def rows_of(j, q):
+        return pl.ds(q * 256 + (240 if j < 0 else (16 - (2 << j)) * ROWS), ROWS if j < 0 else ROWS << j)
+
+    def ship(g, q, j, value):
+        rows, k = rows_of(j, q), 5 * q + j + 1
+        to = xy[(q + j) % 4] if j >= 0 else zs[q - 1]
+        encode(value, sum_code.at[g, rows, :], sum_scale.at[g, k])
+        sums[g, q, j] = (
+            send(sum_code.at[g, rows, :], sum_code_in.at[g, rows, :], to),
+            send(sum_scale.at[g, k], sum_scale_in.at[g, k], to),
+        )
+
+    def arrived(g, q, j):
+        for copy in sums[g, q, j]:
+            copy.wait_recv()
+        return decode_wide(sum_code_in.at[g, rows_of(j, q), :], sum_scale_in.at[g, 5 * q + j + 1])
+
+    def begin(g):
         for q in range(4):
-            sums[name, q, 3] = send(
-                grad.at[pl.ds(LATE + q * CLASS, CLASS), :],
-                recv.at[pl.ds(q * 240, CLASS), :],
-                xy[(q + 3) % 4],
-            )
-
-    def advance(name, grad, recv, zrecv_, j):
+            ship(g, q, 3, grads[g][pl.ds(LATE + q * CLASS, CLASS), :])
+
+    def advance(g, j):
         n = ROWS << j
-        at = (16 - (2 << j)) * ROWS
         for q in range(4):
-            base, low = q * CLASS, q * 240 + at
-            sums[name, q, j].wait_recv()
+            rows = pl.ds(q * CLASS, n)
+            value = grads[g][rows, :] + arrived(g, q, j)
             if j > 0:
-                h = n // 2
-                grad[pl.ds(base + h, h), :] += recv[pl.ds(low + h, h), :]
-                sums[name, q, j - 1] = send(
-                    grad.at[pl.ds(base + h, h), :],
-                    recv.at[pl.ds(low + n, h), :],
-                    xy[(q + j - 1) % 4],
-                )
-                grad[pl.ds(base, h), :] += recv[pl.ds(low, h), :]
+                ship(g, q, j - 1, value[n // 2 :])
+                grads[g][pl.ds(q * CLASS, n // 2), :] = value[: n // 2]
+            elif q > 0:
+                ship(g, q, -1, value)
             else:
-                grad[pl.ds(base, n), :] += recv[pl.ds(low, n), :]
-                if q > 0:
-                    sums[name, q, -1] = send(grad.at[pl.ds(base, n), :], zrecv_.at[q - 1], zs[q - 1])
-
-    def finish(name, grad, zrecv_):
-        total = grad[pl.ds(0, ROWS), :]
+                grads[g][rows, :] = value
+
+    def finish(g):
+        total = grads[g][pl.ds(0, ROWS), :]
         for q in (1, 2, 3):
-            sums[name, q, -1].wait_recv()
-            total = total + zrecv_[q - 1]
+            total = total + arrived(g, q, -1)
         return total
 
     og_swap.wait_recv()
     gd[late, :] = dot(act[late, :], og[...], 1, 1)
-    begin("d", gd, rd)
+    begin(0)
     for q in range(4):
         gathered[1, q, 3].wait_recv()
 
+    pair_swaps = {}
+
+    def exchange(b):
+        core_swaps[b].wait_recv()
+        for i, cols in enumerate(tiles(HALF_TOK)):
+            value = pown[b, :, cols] + precv[b, :, cols]
+            encode(value, pair_code.at[b, :, cols], pair_scale.at[b, :, cols])
+        pair_swaps[b] = (
+            send(pair_code.at[b], pair_code_in.at[1 - b], pair),
+            send(pair_scale.at[b], pair_scale_in.at[1 - b], pair),
+        )
+
+    def complete(b, where, sem):
+        for copy in pair_swaps[1 - b]:
+            copy.wait_recv()
+        for cols in tiles(HALF_TOK):
+            at = pl.ds(b * HALF_TOK + cols.start, 128)
+            near = decode(pair_code.at[b, :, cols], pair_scale.at[b, :, cols], pl.ds(0, 128))
+            far = decode(pair_code_in.at[b, :, cols], pair_scale_in.at[b, :, cols], pl.ds(0, 128))
+            mix[b, :, cols] = (tok[:, at].astype(F32) + (near + far)).astype(BF16)
+        put = pltpu.make_async_copy(mix.at[b], mixed_out.at[:, where], local_sem.at[sem])
+        put.start()
+        return put
+
+    core_swaps = {}
     psend[1] = branch(3)
-    core_swap1 = send(psend.at[1], precv.at[1], core)
+    core_swaps[1] = send(psend.at[1], precv.at[1], core)
     pown[1] = branch(1)
+    exchange(1)
+    psend[0] = branch(2)
+    core_swaps[0] = send(psend.at[0], precv.at[0], core)
     gd[early, :] = dot(act[early, :], og[...], 1, 1)
-    core_swap1.wait_recv()
-    pown[1] += precv[1]
-    pair_swap = send(pown.at[1], zrecv, pair)
+    pown[0] = branch(0)
+    exchange(0)
+    advance(0, 3)
     backward(1)
     gu[late, :] = dot(slope[late, :], nrm[...], 1, 1)
-    begin("u", gu, ru)
-    psend[0] = branch(2)
-    core_swap0 = send(psend.at[0], precv.at[0], core)
-    pown[0] = branch(0)
-    advance("d", gd, rd, zd, 3)
+    begin(1)
+    advance(0, 2)
     backward(0)
     gu[early, :] = dot(slope[early, :], nrm[...], 1, 1)
-    core_swap0.wait_recv()
-    pown[0] += precv[0]
-    advance("d", gd, rd, zd, 2)
-    advance("u", gu, ru, zu, 3)
-    advance("d", gd, rd, zd, 1)
-    advance("u", gu, ru, zu, 2)
+    advance(0, 1)
+    advance(1, 3)
+    advance(0, 0)
+    advance(1, 2)
     moved.wait_recv()
     for i in range(6):
         picked[i] = jnp.where(owner == s, state[i][slot, s], pick_recv[i])
-    advance("d", gd, rd, zd, 0)
-    advance("u", gu, ru, zu, 1)
-
-    pair_swap.wait_recv()
-    mix[0] = (tok[:, first].astype(F32) + (pown[0] + zrecv[...])).astype(BF16)
-    mix_swap = send(mix.at[0], mix.at[1], pair)
-    puts = [pltpu.make_async_copy(mix.at[0], mixed_out.at[:, mine], local_sem.at[10])]
-    puts[0].start()
-    advance("u", gu, ru, zu, 0)
-    fresh[3], fresh[4], fresh[5] = adam_update(picked[1], picked[3], picked[5], finish("d", gd, zd))
-    fresh[0], fresh[1], fresh[2] = adam_update(picked[0], picked[2], picked[4], finish("u", gu, zu))
+    advance(1, 1)
+    puts = [complete(0, mine, 11)]
+    advance(1, 0)
+    fresh[3], fresh[4], fresh[5] = adam_update(picked[1], picked[3], picked[5], finish(0))
+    fresh[0], fresh[1], fresh[2] = adam_update(picked[0], picked[2], picked[4], finish(1))
     puts.append(pltpu.make_async_copy(fresh, state_out, local_sem.at[12]))
     puts[1].start()
-    mix_swap.wait_recv()
-    puts.append(pltpu.make_async_copy(mix.at[1], mixed_out.at[:, other], local_sem.at[11]))
-    puts[2].start()
+    puts.append(complete(1, other, 10))
     for copy in puts:
         copy.wait()
     for copy in started:
         copy.wait_send()
 
 
-COPIES = 7 + 1 + 2 + 1 + 32 + 4 + 38
+COPIES = 2 + 6 + 1 + 2 + 1 + 32 + 2 + 4 + 2 * 38
 
 
 def hand_out(mixed_in, state_in, mixed_out, *rest):
-    outs, sem = rest[:6], rest[6]
-    copies = [pltpu.make_async_copy(mixed_in, mixed_out, sem.at[6])]
-    copies += [pltpu.make_async_copy(state_in.at[i], outs[i], sem.at[i]) for i in range(6)]
-    for copy in copies:
-        copy.start()
-    for copy in copies:
-        copy.wait()
+    outs, (mixed, state, sem) = rest[:6], rest[6:]
+    bands = [pl.ds(i * D // 4, D // 4) for i in range(4)]
+    gets = [pltpu.make_async_copy(mixed_in.at[band, :], mixed.at[band, :], sem.at[i]) for i, band in enumerate(bands)]
+    gets.append(pltpu.make_async_copy(state_in, state, sem.at[4]))
+    puts = [[pltpu.make_async_copy(mixed.at[band, :], mixed_out.at[band, :], sem.at[5 + i])] for i, band in enumerate(bands)]
+    puts.append([pltpu.make_async_copy(state.at[i], outs[i], sem.at[9 + i]) for i in range(6)])
+    for get in gets:
+        get.start()
+    for get, put in zip(gets, puts):
+        get.wait()
+        for copy in put:
+            copy.start()
+    for put in puts:
+        for copy in put:
+            copy.wait()
 
 
 def local(tokens, out_grad, boundary, up_old, down_old, up_mom, up_var, down_mom, down_var):
@@ -384,7 +445,7 @@
         scratch_shapes=[
             *[V((layers, 2, ROWS, D), F32)] * 6,
             V((2, 2, ROWS, D), BF16),
-            V((7, 2, ROWS, D), BF16),
+            V((2, ROWS, D), BF16),
             V((6, ROWS, D), F32),
             V((6, ROWS, D), F32),
             V((6, ROWS, D), F32),
@@ -400,14 +461,11 @@
             V((2, D, HALF_TOK), F32),
             V((2, D, HALF_TOK), F32),
             V((2, D, HALF_TOK), F32),
-            V((D, HALF_TOK), F32),
+            *[V((2, D, HALF_TOK), jnp.int16), V((2, 8, HALF_TOK), F32)] * 2,
             V((2, D, HALF_TOK), BF16),
             V((UNITS, D), F32),
             V((UNITS, D), F32),
-            V((4 * 240, D), F32),
-            V((4 * 240, D), F32),
-            V((3, ROWS, D), F32),
-            V((3, ROWS, D), F32),
+            *[V((2, 4 * 256, D), jnp.int16), V((2, 20, 8, 128), F32)] * 2,
             pltpu.SemaphoreType.DMA((13,)),
             pltpu.SemaphoreType.DMA((COPIES,)),
             pltpu.SemaphoreType.DMA((COPIES,)),
@@ -432,7 +490,7 @@
         out_shape=[mixed_type] + [jax.ShapeDtypeStruct((ROWS, D), F32)] * 6,
         in_specs=[hbm] * 2,
         out_specs=[hbm] * 7,
-        scratch_shapes=[pltpu.SemaphoreType.DMA((7,))],
+        scratch_shapes=[V((D, TOK), BF16), V((6, ROWS, D), F32), pltpu.SemaphoreType.DMA((15,))],
         compiler_params=pltpu.CompilerParams(vmem_limit_bytes=60 * 2**20),
         name="hand_out",
     )(*results)

time: 165 us -> 90.9 us (0.55)
  Pallas kernels: 162 us -> 88.8 us
    pallas_call x1, Pallas kernels: 50.3 us -> 2.24 us  [local(): pl.pallas_call(hand_out, out_shape=[mixed_type] + [jax.ShapeDtypeStruct((...]
    pallas_call x1, Pallas kernels: 112 us -> 86.5 us  [local(): pl.pallas_call(kernel, out_shape=[mixed_type, jax.ShapeDtypeStruct((6, RO...]
where the time goes in v3:
time: 90.9 us; the launch traced here: 90.2 us
  Pallas kernels  88.8 us (98%)
  between operations  1.45 us (2%)
    pallas_call x1, Pallas kernels, local(): pl.pallas_call(kernel, out_shape=[mixed_type, jax.ShapeDtypeStruct((6, RO...  86.5 us
    pallas_call x1, Pallas kernels, local(): pl.pallas_call(hand_out, out_shape=[mixed_type] + [jax.ShapeDtypeStruct((...  2.24 us

profile of v3, /device:TPU:1, one launch (start us, length us, event | category | flops | bytes accessed | tf_op | source)
XLA Modules:
  0.0 90.2 jit_solution(4381998011669066082)
XLA Ops:
  1.3 86.5 %block_step.1 = (bf16[832,768]{1,0:T(8,128)(2,1)}, f32[6,16,832]{2,1,0:T(8,128)}) custom-call(s32[1]{0:T(128)S(6)} %copy.16.boundary, bf16[832,768]{1,0:T(8,128)(2,1)} %bitcast.18, bf16[832,768]{1,0:T(8,128)(2,1)} %bitcast.19, f32[6,2,16,832]{3,2,1,0:T(8,128)} %bitcast.20, f32[6,2,16,832]{3,2,1,0:T(8,128)} %down_w_in.1, f32[6,2,16,832]{3,2,1,0:T(8,128)} %bitcast.21, ...), custom_call_target="tpu_custom_call" | custom-call | tf_op jit(solution)/shard_map/block_step/pallas_call | solution.py:440
  87.8 2.2 %hand_out.1 = (bf16[832,768]{1,0:T(8,128)(2,1)}, f32[16,832]{1,0:T(8,128)}, f32[16,832]{1,0:T(8,128)}, f32[16,832]{1,0:T(8,128)}, f32[16,832]{1,0:T(8,128)}, /*index=5*/f32[16,832]{1,0:T(8,128)}, f32[16,832]{1,0:T(8,128)}) custom-call(bf16[832,768]{1,0:T(8,128)(2,1)} %get-tuple-element.16.mixed_in, f32[6,16,832]{2,1,0:T(8,128)} %get-tuple-element.17.state_in), custom_call_target="tpu_custom_call" | custom-call | tf_op jit(solution)/shard_map/hand_out/pallas_call | solution.py:488

commit v4 on v3

--- a/solution.py
+++ b/solution.py
@@ -224,16 +224,36 @@
         copy.wait()
     weights = (w1, w2)
     gathered = {}
+    arrivals = {}
+
+    def row_of(q, slot_):
+        return q * CLASS + (slot_ * ROWS if slot_ < 8 else LATE + (slot_ - 8) * ROWS)
 
     def spread(m, q, j):
-        n, at = ROWS << j, q * CLASS
-        if j > 0 or q > 0:
-            gathered[m, q, j - 1].wait_recv()
-        gathered[m, q, j] = send(
-            weights[m].at[pl.ds(at, n), :],
-            weights[m].at[pl.ds(at + n if j < 3 else LATE + at, n), :],
-            xy[(q + j) % 4],
-        )
+        if j == 0:
+            if q > 0:
+                gathered[m, q, -1].wait_recv()
+            low, size = 0, 1
+        else:
+            low = size = 1 << (j - 1)
+            for copy in arrivals[m, q, j - 1]:
+                copy.wait_recv()
+        for k in range(j, 4):
+            copy = send(
+                weights[m].at[pl.ds(row_of(q, low), size * ROWS), :],
+                weights[m].at[pl.ds(row_of(q, (1 << k) + low), size * ROWS), :],
+                xy[(q + k) % 4],
+            )
+            arrivals.setdefault((m, q, k), []).append(copy)
+
+    def spread_all(m, j):
+        for q in range(4):
+            spread(m, q, j)
+
+    def all_here(m, j):
+        for q in range(4):
+            for copy in arrivals[m, q, j]:
+                copy.wait_recv()
 
     for m in (0, 1):
         offers[m].wait_recv()
@@ -242,34 +262,29 @@
             gathered[m, q, -1] = send(
                 weights[m].at[pl.ds(0, ROWS), :], weights[m].at[pl.ds(q * CLASS, ROWS), :], zs[q - 1]
             )
-        spread(m, 0, 0)
     for copy in get_og:
         copy.wait()
     og_swap = send(og.at[:, pl.ds(0, TOK)], og.at[:, pl.ds(TOK, TOK)], core)
     norm(0)
-    for m in (0, 1):
-        for q in (1, 2, 3):
-            spread(m, q, 0)
+    spread_all(0, 0)
     norm(1)
+    spread_all(0, 1)
     norm(2)
     nrm_swaps = [send(nrm.at[:, first], nrm.at[:, pl.ds(TOK, HALF_TOK)], core)]
-    for m in (0, 1):
-        for q in range(4):
-            spread(m, q, 1)
+    spread_all(1, 0)
     norm(3)
+    spread_all(0, 2)
+    norm(4)
+    norm(5)
+    nrm_swaps.append(send(nrm.at[:, second], nrm.at[:, pl.ds(TOK + HALF_TOK, HALF_TOK)], core))
+    spread_all(1, 1)
+    spread_all(0, 3)
     for copy in get_mv:
         copy.wait()
     for i in range(6):
         pick_send[i] = state[i][slot, 1 - s]
     moved = send(pick_send, pick_recv, pair)
-    norm(4)
-    for m in (0, 1):
-        for q in range(4):
-            spread(m, q, 2)
-    norm(5)
-    nrm_swaps.append(send(nrm.at[:, second], nrm.at[:, pl.ds(TOK + HALF_TOK, HALF_TOK)], core))
-    for q in range(4):
-        spread(0, q, 3)
+    spread_all(1, 2)
 
     def forward(part, t):
         rows, cols = pl.ds(part * LATE, LATE), pl.ds(t * TOK, TOK)
@@ -286,17 +301,6 @@
 
     def branch(block):
         return dot(w2[...], act[:, pl.ds(block * HALF_TOK, HALF_TOK)], 0, 0)
-
-    forward(0, 0)
-    for copy in nrm_swaps:
-        copy.wait_recv()
-    forward(0, 1)
-    for q in range(4):
-        gathered[0, q, 3].wait_recv()
-    for q in range(4):
-        spread(1, q, 3)
-    forward(1, 0)
-    forward(1, 1)
 
     sums = {}
     grads = (gd, gu)
@@ -342,11 +346,19 @@
             total = total + arrived(g, q, -1)
         return total
 
+    forward(0, 0)
+    for copy in nrm_swaps:
+        copy.wait_recv()
+    forward(0, 1)
+    spread_all(1, 3)
     og_swap.wait_recv()
+    gd[early, :] = dot(act[early, :], og[...], 1, 1)
+    all_here(0, 3)
+    forward(1, 0)
+    forward(1, 1)
     gd[late, :] = dot(act[late, :], og[...], 1, 1)
     begin(0)
-    for q in range(4):
-        gathered[1, q, 3].wait_recv()
+    all_here(1, 3)
 
     pair_swaps = {}
 
@@ -376,18 +388,17 @@
     psend[1] = branch(3)
     core_swaps[1] = send(psend.at[1], precv.at[1], core)
     pown[1] = branch(1)
+    backward(1)
     exchange(1)
+    gu[late, :] = dot(slope[late, :], nrm[...], 1, 1)
+    begin(1)
     psend[0] = branch(2)
     core_swaps[0] = send(psend.at[0], precv.at[0], core)
-    gd[early, :] = dot(act[early, :], og[...], 1, 1)
+    advance(0, 3)
     pown[0] = branch(0)
     exchange(0)
-    advance(0, 3)
-    backward(1)
-    gu[late, :] = dot(slope[late, :], nrm[...], 1, 1)
-    begin(1)
+    backward(0)
     advance(0, 2)
-    backward(0)
     gu[early, :] = dot(slope[early, :], nrm[...], 1, 1)
     advance(0, 1)
     advance(1, 3)
@@ -410,7 +421,7 @@
         copy.wait_send()
 
 
-COPIES = 2 + 6 + 1 + 2 + 1 + 32 + 2 + 4 + 2 * 38
+COPIES = 2 + 6 + 1 + 2 + 1 + 80 + 2 + 4 + 2 * 38
 
 
 def hand_out(mixed_in, state_in, mixed_out, *rest):

time: 90.9 us -> 92.9 us (1.022)
  Pallas kernels: 88.8 us -> 91.3 us
    pallas_call x1, Pallas kernels: 86.5 us -> 89.1 us  [local(): pl.pallas_call(kernel, out_shape=[mixed_type, jax.ShapeDtypeStruct((6, RO...]
where the time goes in v4:
time: 92.9 us; the launch traced here: 92.8 us
  Pallas kernels  91.3 us (98%)
  between operations  1.45 us (2%)
    pallas_call x1, Pallas kernels, local(): pl.pallas_call(kernel, out_shape=[mixed_type, jax.ShapeDtypeStruct((6, RO...  89.1 us
    pallas_call x1, Pallas kernels, local(): pl.pallas_call(hand_out, out_shape=[mixed_type] + [jax.ShapeDtypeStruct((...  2.24 us

profile of v4, /device:TPU:1, one launch (start us, length us, event | category | flops | bytes accessed | tf_op | source)
XLA Modules:
  0.0 92.8 jit_solution(9517571789044407370)
XLA Ops:
  1.3 89.1 %block_step.1 = (bf16[832,768]{1,0:T(8,128)(2,1)}, f32[6,16,832]{2,1,0:T(8,128)}) custom-call(s32[1]{0:T(128)S(6)} %copy.16.boundary, bf16[832,768]{1,0:T(8,128)(2,1)} %bitcast.18, bf16[832,768]{1,0:T(8,128)(2,1)} %bitcast.19, f32[6,2,16,832]{3,2,1,0:T(8,128)} %bitcast.20, f32[6,2,16,832]{3,2,1,0:T(8,128)} %down_w_in.1, f32[6,2,16,832]{3,2,1,0:T(8,128)} %bitcast.21, ...), custom_call_target="tpu_custom_call" | custom-call | tf_op jit(solution)/shard_map/block_step/pallas_call | solution.py:451
  90.4 2.2 %hand_out.1 = (bf16[832,768]{1,0:T(8,128)(2,1)}, f32[16,832]{1,0:T(8,128)}, f32[16,832]{1,0:T(8,128)}, f32[16,832]{1,0:T(8,128)}, f32[16,832]{1,0:T(8,128)}, /*index=5*/f32[16,832]{1,0:T(8,128)}, f32[16,832]{1,0:T(8,128)}) custom-call(bf16[832,768]{1,0:T(8,128)(2,1)} %get-tuple-element.16.mixed_in, f32[6,16,832]{2,1,0:T(8,128)} %get-tuple-element.17.state_in), custom_call_target="tpu_custom_call" | custom-call | tf_op jit(solution)/shard_map/hand_out/pallas_call | solution.py:499

commit v5 on v4

--- a/solution.py
+++ b/solution.py
@@ -265,26 +265,26 @@
     for copy in get_og:
         copy.wait()
     og_swap = send(og.at[:, pl.ds(0, TOK)], og.at[:, pl.ds(TOK, TOK)], core)
+    spread_all(0, 0)
     norm(0)
-    spread_all(0, 0)
+    spread_all(1, 0)
     norm(1)
     spread_all(0, 1)
     norm(2)
     nrm_swaps = [send(nrm.at[:, first], nrm.at[:, pl.ds(TOK, HALF_TOK)], core)]
-    spread_all(1, 0)
+    spread_all(1, 1)
     norm(3)
     spread_all(0, 2)
     norm(4)
     norm(5)
     nrm_swaps.append(send(nrm.at[:, second], nrm.at[:, pl.ds(TOK + HALF_TOK, HALF_TOK)], core))
-    spread_all(1, 1)
-    spread_all(0, 3)
+    spread_all(1, 2)
     for copy in get_mv:
         copy.wait()
     for i in range(6):
         pick_send[i] = state[i][slot, 1 - s]
     moved = send(pick_send, pick_recv, pair)
-    spread_all(1, 2)
+    spread_all(0, 3)
 
     def forward(part, t):
         rows, cols = pl.ds(part * LATE, LATE), pl.ds(t * TOK, TOK)
@@ -299,8 +299,8 @@
             back = dot(w2[rows, :], og[:, cols], 1, 0)
             slope[rows, cols] = (back * gate[rows, cols]).astype(BF16)
 
-    def branch(block):
-        return dot(w2[...], act[:, pl.ds(block * HALF_TOK, HALF_TOK)], 0, 0)
+    def branch(block, rows=pl.ds(0, UNITS)):
+        return dot(w2[rows, :], act[rows, pl.ds(block * HALF_TOK, HALF_TOK)], 0, 0)
 
     sums = {}
     grads = (gd, gu)
@@ -353,6 +353,8 @@
     spread_all(1, 3)
     og_swap.wait_recv()
     gd[early, :] = dot(act[early, :], og[...], 1, 1)
+    psend[1] = branch(3, early)
+    pown[1] = branch(1, early)
     all_here(0, 3)
     forward(1, 0)
     forward(1, 1)
@@ -385,11 +387,11 @@
         return put
 
     core_swaps = {}
-    psend[1] = branch(3)
+    psend[1] += branch(3, late)
     core_swaps[1] = send(psend.at[1], precv.at[1], core)
-    pown[1] = branch(1)
+    pown[1] += branch(1, late)
+    exchange(1)
     backward(1)
-    exchange(1)
     gu[late, :] = dot(slope[late, :], nrm[...], 1, 1)
     begin(1)
     psend[0] = branch(2)
@@ -398,18 +400,18 @@
     pown[0] = branch(0)
     exchange(0)
     backward(0)
+    gu[early, :] = dot(slope[early, :], nrm[...], 1, 1)
+    advance(1, 3)
     advance(0, 2)
-    gu[early, :] = dot(slope[early, :], nrm[...], 1, 1)
+    advance(1, 2)
     advance(0, 1)
-    advance(1, 3)
+    advance(1, 1)
     advance(0, 0)
-    advance(1, 2)
+    advance(1, 0)
     moved.wait_recv()
     for i in range(6):
         picked[i] = jnp.where(owner == s, state[i][slot, s], pick_recv[i])
-    advance(1, 1)
     puts = [complete(0, mine, 11)]
-    advance(1, 0)
     fresh[3], fresh[4], fresh[5] = adam_update(picked[1], picked[3], picked[5], finish(0))
     fresh[0], fresh[1], fresh[2] = adam_update(picked[0], picked[2], picked[4], finish(1))
     puts.append(pltpu.make_async_copy(fresh, state_out, local_sem.at[12]))

time: 92.9 us -> 90.3 us (0.972)
  Pallas kernels: 91.3 us -> 88.8 us
    pallas_call x1, Pallas kernels: 89.1 us -> 86.5 us  [local(): pl.pallas_call(kernel, out_shape=[mixed_type, jax.ShapeDtypeStruct((6, RO...]
where the time goes in v5:
time: 90.3 us; the launch traced here: 90.2 us
  Pallas kernels  88.8 us (98%)
  between operations  1.45 us (2%)
    pallas_call x1, Pallas kernels, local(): pl.pallas_call(kernel, out_shape=[mixed_type, jax.ShapeDtypeStruct((6, RO...  86.5 us
    pallas_call x1, Pallas kernels, local(): pl.pallas_call(hand_out, out_shape=[mixed_type] + [jax.ShapeDtypeStruct((...  2.24 us

profile of v5, /device:TPU:1, one launch (start us, length us, event | category | flops | bytes accessed | tf_op | source)
XLA Modules:
  0.0 90.2 jit_solution(14942124797979599814)
XLA Ops:
  1.3 86.5 %block_step.1 = (bf16[832,768]{1,0:T(8,128)(2,1)}, f32[6,16,832]{2,1,0:T(8,128)}) custom-call(s32[1]{0:T(128)S(6)} %copy.16.boundary, bf16[832,768]{1,0:T(8,128)(2,1)} %bitcast.18, bf16[832,768]{1,0:T(8,128)(2,1)} %bitcast.19, f32[6,2,16,832]{3,2,1,0:T(8,128)} %bitcast.20, f32[6,2,16,832]{3,2,1,0:T(8,128)} %down_w_in.1, f32[6,2,16,832]{3,2,1,0:T(8,128)} %bitcast.21, ...), custom_call_target="tpu_custom_call" | custom-call | tf_op jit(solution)/shard_map/block_step/pallas_call | solution.py:453
  87.8 2.2 %hand_out.1 = (bf16[832,768]{1,0:T(8,128)(2,1)}, f32[16,832]{1,0:T(8,128)}, f32[16,832]{1,0:T(8,128)}, f32[16,832]{1,0:T(8,128)}, f32[16,832]{1,0:T(8,128)}, /*index=5*/f32[16,832]{1,0:T(8,128)}, f32[16,832]{1,0:T(8,128)}) custom-call(bf16[832,768]{1,0:T(8,128)(2,1)} %get-tuple-element.16.mixed_in, f32[6,16,832]{2,1,0:T(8,128)} %get-tuple-element.17.state_in), custom_call_target="tpu_custom_call" | custom-call | tf_op jit(solution)/shard_map/hand_out/pallas_call | solution.py:501

commit v6 on v5

--- a/solution.py
+++ b/solution.py
@@ -358,8 +358,6 @@
     all_here(0, 3)
     forward(1, 0)
     forward(1, 1)
-    gd[late, :] = dot(act[late, :], og[...], 1, 1)
-    begin(0)
     all_here(1, 3)
 
     pair_swaps = {}
@@ -369,10 +367,12 @@
         for i, cols in enumerate(tiles(HALF_TOK)):
             value = pown[b, :, cols] + precv[b, :, cols]
             encode(value, pair_code.at[b, :, cols], pair_scale.at[b, :, cols])
-        pair_swaps[b] = (
-            send(pair_code.at[b], pair_code_in.at[1 - b], pair),
-            send(pair_scale.at[b], pair_scale_in.at[1 - b], pair),
-        )
+        pair_swaps[b] = [send(pair_scale.at[b], pair_scale_in.at[1 - b], pair)]
+
+    def hand_over(b, first_, count_):
+        for k in range(first_, first_ + count_):
+            rows = pl.ds(k * 64, 64)
+            pair_swaps[b].append(send(pair_code.at[b, rows, :], pair_code_in.at[1 - b, rows, :], pair))
 
     def complete(b, where, sem):
         for copy in pair_swaps[1 - b]:
@@ -390,7 +390,10 @@
     psend[1] += branch(3, late)
     core_swaps[1] = send(psend.at[1], precv.at[1], core)
     pown[1] += branch(1, late)
+    gd[late, :] = dot(act[late, :], og[...], 1, 1)
     exchange(1)
+    hand_over(1, 0, 13)
+    begin(0)
     backward(1)
     gu[late, :] = dot(slope[late, :], nrm[...], 1, 1)
     begin(1)
@@ -399,15 +402,21 @@
     advance(0, 3)
     pown[0] = branch(0)
     exchange(0)
+    hand_over(0, 0, 4)
     backward(0)
     gu[early, :] = dot(slope[early, :], nrm[...], 1, 1)
     advance(1, 3)
+    hand_over(0, 4, 3)
     advance(0, 2)
     advance(1, 2)
+    hand_over(0, 7, 3)
     advance(0, 1)
     advance(1, 1)
+    hand_over(0, 10, 1)
     advance(0, 0)
+    hand_over(0, 11, 1)
     advance(1, 0)
+    hand_over(0, 12, 1)
     moved.wait_recv()
     for i in range(6):
         picked[i] = jnp.where(owner == s, state[i][slot, s], pick_recv[i])
@@ -423,7 +432,7 @@
         copy.wait_send()
 
 
-COPIES = 2 + 6 + 1 + 2 + 1 + 80 + 2 + 4 + 2 * 38
+COPIES = 24 + 2 + 6 + 1 + 2 + 1 + 80 + 2 + 4 + 2 * 38
 
 
 def hand_out(mixed_in, state_in, mixed_out, *rest):

time: 90.3 us -> 89.4 us (0.990)
  Pallas kernels: 88.8 us -> 87.8 us
    pallas_call x1, Pallas kernels: 86.5 us -> 85.6 us  [local(): pl.pallas_call(kernel, out_shape=[mixed_type, jax.ShapeDtypeStruct((6, RO...]
where the time goes in v6:
time: 89.4 us; the launch traced here: 89.3 us
  Pallas kernels  87.8 us (98%)
  between operations  1.45 us (2%)
    pallas_call x1, Pallas kernels, local(): pl.pallas_call(kernel, out_shape=[mixed_type, jax.ShapeDtypeStruct((6, RO...  85.6 us
    pallas_call x1, Pallas kernels, local(): pl.pallas_call(hand_out, out_shape=[mixed_type] + [jax.ShapeDtypeStruct((...  2.24 us

profile of v6, /device:TPU:1, one launch (start us, length us, event | category | flops | bytes accessed | tf_op | source)
XLA Modules:
  0.0 89.3 jit_solution(1741419816585575423)
XLA Ops:
  1.3 85.6 %block_step.1 = (bf16[832,768]{1,0:T(8,128)(2,1)}, f32[6,16,832]{2,1,0:T(8,128)}) custom-call(s32[1]{0:T(128)S(6)} %copy.16.boundary, bf16[832,768]{1,0:T(8,128)(2,1)} %bitcast.18, bf16[832,768]{1,0:T(8,128)(2,1)} %bitcast.19, f32[6,2,16,832]{3,2,1,0:T(8,128)} %bitcast.20, f32[6,2,16,832]{3,2,1,0:T(8,128)} %down_w_in.1, f32[6,2,16,832]{3,2,1,0:T(8,128)} %bitcast.21, ...), custom_call_target="tpu_custom_call" | custom-call | tf_op jit(solution)/shard_map/block_step/pallas_call | solution.py:462
  86.9 2.2 %hand_out.1 = (bf16[832,768]{1,0:T(8,128)(2,1)}, f32[16,832]{1,0:T(8,128)}, f32[16,832]{1,0:T(8,128)}, f32[16,832]{1,0:T(8,128)}, f32[16,832]{1,0:T(8,128)}, /*index=5*/f32[16,832]{1,0:T(8,128)}, f32[16,832]{1,0:T(8,128)}) custom-call(bf16[832,768]{1,0:T(8,128)(2,1)} %get-tuple-element.16.mixed_in, f32[6,16,832]{2,1,0:T(8,128)} %get-tuple-element.17.state_in), custom_call_target="tpu_custom_call" | custom-call | tf_op jit(solution)/shard_map/hand_out/pallas_call | solution.py:510
